TPU v7x, 32 devices: a whole 2x2x4 slice. The times are simulated.
32 devices in a mesh: grp: 2 (over y), pair: 8 (over z, core), seg: 2 (over x), lag: 1.
Axes of the slice: x: 2, y: 2, z: 4, core: 2. Of those that a mesh axis runs over, the one named last changes fastest.
Arguments:
- strain: float32 [4096, 1024], P(('grp', 'pair'), 'seg'), parts along dimension 0, may hold values from -1000 to 1000, as said below
- block_slot: int32 [32], P('grp'), parts along dimension 0, may hold values from 0 to 15, as said below
- pair_blocks: int32 [128, 2], P('grp'), parts along dimension 0, may hold values from 0 to 15, as said below
Outputs:
- stacks: float32 [128, 400, 128], P(('grp', 'pair', 'seg'), 'lag'), parts along dimension 0
There are 2 independent parts, one for each index of `grp`. A program takes and returns all parts, laid end to end along the dimension named above; each array names one. Nothing has to cross between parts.
Inputs may be any that keep to these rules, and one draw needn't show every extreme that they name: A permutation; block b is held by index block_slot[b] // 2 of pair. `pair_blocks`: rows p * 8 to (p + 1) * 8 - 1 are the pairs of index p of pair; together they name 16 distinct blocks; no index of pair holds more than 2 of them, and some index holds exactly 2. `strain`: channel gains and envelopes differ widely.
All inputs are finite; a program needn't handle non-finite values.
Results may differ from a plain program's by a relative error of at most 0.006.
Values may be sent and summed in bfloat16 or wider, within the bound.
A program may use at most 64 MiB of HBM per device.

v0:
```python
import math

import jax
import jax.numpy as jnp
from jax import lax
from jax.sharding import PartitionSpec as P

CHB = 128
WIN = 512
MAXLAG = 200
HALF = 64
LAGS = 400


EPS = 1e-06


def make_tables(freq_part, lag_count):
    half_bins = WIN // lag_count
    length = 2 * WIN
    freq = freq_part * half_bins + jnp.arange(half_bins, dtype=jnp.int32)
    times = jnp.arange(WIN, dtype=jnp.int32)
    first_bin = freq == 0
    angle = (times[:, None] * freq[None, :] % length).astype(jnp.float32) * (2.0 * math.pi / length)
    alternate = (1 - 2 * (times % 2)).astype(jnp.float32)
    sine = jnp.where(first_bin[None, :], alternate[:, None], jnp.sin(angle))
    forward = jnp.concatenate([jnp.cos(angle), sine], axis=1)
    forward_high = forward.astype(jnp.bfloat16)
    forward_low = (forward - forward_high.astype(jnp.float32)).astype(jnp.bfloat16)
    shifts = jnp.arange(LAGS, dtype=jnp.int32) - MAXLAG
    back_angle = (freq[:, None] * shifts[None, :] % length).astype(jnp.float32) * (
        2.0 * math.pi / length
    )
    weight = jnp.where(first_bin, 1.0, 2.0).astype(jnp.float32)[:, None]
    upper = weight * jnp.cos(back_angle) / length
    lag_sign = (1 - 2 * (shifts % 2)).astype(jnp.float32)
    lower = jnp.where(
        first_bin[:, None], lag_sign[None, :] / length, -2.0 * jnp.sin(back_angle) / length
    )
    inverse = jnp.concatenate([upper, lower], axis=0)
    keep = (freq > 0).astype(jnp.float32)
    return ((forward_high, forward_low), inverse, keep)


def spectra(blocks, tables):
    high = jnp.einsum("bcst,tk->bcsk", blocks, tables[0], preferred_element_type=jnp.float32)
    low = jnp.einsum("bcst,tk->bcsk", blocks, tables[1], preferred_element_type=jnp.float32)
    return high + low


def cross_stack(first, second, keep, half_bins):
    first_re, first_im = (first[..., :half_bins], first[..., half_bins:])
    second_re, second_im = (second[..., :half_bins], second[..., half_bins:])
    real_part = first_re * second_re + keep * first_im * second_im
    imag_part = (
        keep * (first_im * second_re - first_re * second_im) + (1.0 - keep) * first_im * second_im
    )
    return jnp.sum(jnp.concatenate([real_part, imag_part], axis=-1), axis=2)


def to_lags(cross, inverse):
    return jnp.einsum("pck,kl->plc", cross, inverse, precision=lax.Precision.HIGHEST)


def shards(strain, block_slot, pair_blocks):
    pair_count = lax.axis_size("pair")
    seg_count = lax.axis_size("seg")
    lag_count = lax.axis_size("lag")
    holder = lax.axis_index("pair")
    freq_part = lax.axis_index("lag")
    blk_dev = strain.shape[0] // CHB
    seg_dev = strain.shape[1] // WIN
    nblk = block_slot.shape[0]
    pairs_dev = pair_blocks.shape[0] // pair_count
    refs = 2 * pairs_dev
    capacity = (refs + pair_count - 1) // pair_count
    half_bins = WIN // lag_count
    scale = 1.0 / math.sqrt(seg_dev * seg_count * WIN)
    series = strain.reshape(blk_dev, CHB, seg_dev, WIN)
    times = jnp.arange(WIN, dtype=jnp.int32)
    band = (jnp.abs(times[:, None] - times[None, :]) <= HALF).astype(jnp.float32)
    count = jnp.sum(band, axis=0)
    sums = jnp.einsum("bcst,tu->bcsu", jnp.abs(series), band, precision=lax.Precision.HIGHEST)
    normed = (series / (sums / count + EPS)).astype(jnp.bfloat16)
    tables, inverse, keep = make_tables(freq_part, lag_count)
    catalog = jnp.arange(nblk, dtype=jnp.int32)
    wanted = pair_blocks.reshape(pair_count, refs)
    hits = (wanted[:, :, None] == catalog[None, None, :]).astype(jnp.int32)
    ref_slot = jnp.sum(hits * block_slot[None, None, :], axis=2)
    ref_owner = ref_slot // blk_dev
    ref_local = ref_slot % blk_dev
    ordering = jnp.arange(refs, dtype=jnp.int32)
    earlier = ordering[:, None] > ordering[None, :]
    ref_rank = jnp.sum(
        ((ref_owner[:, :, None] == ref_owner[:, None, :]) & earlier[None, :, :]).astype(jnp.int32),
        axis=2,
    )
    mine = ref_owner == holder
    rank_hot = (
        (ref_rank[:, :, None] == jnp.arange(capacity, dtype=jnp.int32)[None, None, :])
        & mine[:, :, None]
    ).astype(jnp.float32)
    local_hot = (
        ref_local[:, :, None] == jnp.arange(blk_dev, dtype=jnp.int32)[None, None, :]
    ).astype(jnp.float32)
    select = jnp.einsum("dkr,dkl->drl", rank_hot, local_hot)
    my_owner = lax.dynamic_index_in_dim(ref_owner, holder, 0, keepdims=False)
    my_rank = lax.dynamic_index_in_dim(ref_rank, holder, 0, keepdims=False)
    position = my_owner * capacity + my_rank
    payload = normed.reshape(blk_dev, CHB * seg_dev * WIN)
    outgoing = jnp.einsum(
        "drl,lx->drx", select.astype(jnp.bfloat16), payload, preferred_element_type=jnp.float32
    ).astype(jnp.bfloat16)
    incoming = lax.all_to_all(outgoing, "pair", split_axis=0, concat_axis=0, tiled=True)
    picked = jnp.take(
        incoming.reshape(pair_count * capacity, CHB * seg_dev * WIN), position, axis=0
    )
    picked_spectra = spectra(picked.reshape(refs, CHB, seg_dev, WIN), tables)
    paired = picked_spectra.reshape(pairs_dev, 2, CHB, seg_dev, 2 * half_bins)
    cross = cross_stack(paired[:, 0], paired[:, 1], keep, half_bins)
    partial_lags = to_lags(cross, inverse)
    lag_part = lax.psum_scatter(partial_lags, "lag", scatter_dimension=1, tiled=True)
    stacked = lax.psum_scatter(lag_part, "seg", scatter_dimension=0, tiled=True)
    return stacked * scale


def solution(mesh):
    in_specs = (P(("grp", "pair"), "seg"), P("grp"), P("grp", None))
    out_specs = P(("grp", "pair", "seg"), "lag", None)
    return jax.shard_map(shards, mesh=mesh, in_specs=in_specs, out_specs=out_specs, check_vma=False)
```

profile of v0, /device:TPU:9, one launch (start us, length us, event | category | flops | bytes accessed | tf_op | source)
XLA Modules:
  0.0 128.9 jit_solution(13397535168224393091)
XLA Ops:
  6.5 0.2 convert_reduce_fusion
  6.7 0.8 copy.21
  7.5 0.1 eq.93
  7.6 0.9 select_reduce_fusion
  8.5 1.2 copy.22
  9.8 1.7 %fusion.10 = bf16[2,128,512]{1,2,0:T(8,128)(2,1)S(1)} fusion(f32[2,128,512]{1,2,0:T(8,128)S(1)} %copy.22, f32[2,128,512]{2,1,0:T(8,128)} %bitcast.52, f32[512]{0:T(512)S(1)} %convert_reduce_fusion), kind=kOutput, calls=%fused_computation.29 | convolution fusion | flops 806748160 | bytes 1312768 | tf_op jit(solution)/shard_map/bcst,tu->bcsu/dot_general | solution.py:83
  11.5 0.1 copy.23
  11.7 0.2 reshape.222
  11.9 0.3 convert_reduce_fusion.1
  12.2 0.1 convolution_convert_fusion.1
  12.3 0.7 convolution_convert_fusion
  13.0 3.5 %copy.25 = bf16[8,2,65536]{2,1,0:T(2,128)(2,1)} copy(bf16[8,2,65536]{2,0,1:T(8,128)(2,1)S(1)} %convolution_convert_fusion) | data formatting | bytes 4194304 | tf_op jit(solution)/shard_map/convert_element_type | solution.py:113
  16.5 5.6 %all-to-all-start = ((bf16[8,2,65536]{2,1,0:T(2,128)(2,1)}), bf16[8,2,65536]{2,1,0:T(2,128)(2,1)}, u32[]{:S(2)}, u32[]{:S(2)}) async-start(bf16[8,2,65536]{2,1,0:T(2,128)(2,1)} %copy.25), calls=%async_computation | async-start | bytes 4194304 | tf_op jit(solution)/shard_map/all_to_all | solution.py:114
  22.1 0.0 reduce-scatter.2.cloned.1.call-start
  22.2 4.6 %multiply_multiply_fusion = (f32[512,400]{0,1:T(8,128)}, f32[512,400]{0,1:T(8,128)}) fusion(s32[400]{0:T(512)S(1)} %iota_add_fusion, f32[512]{0:T(512)S(1)} %broadcast_select_fusion, f32[400]{0:T(512)S(1)} %fusion.45, pred[512]{0:T(512)(128)(4,1)S(1)} %iota_compare_fusion.3), kind=kLoop, calls=%fused_computation.48 | loop fusion | flops 3686400 | bytes 1644160 | tf_op jit(solution)/shard_map/div | solution.py:35
  26.8 4.9 %sine_select_fusion = (f32[512,512]{1,0:T(8,128)S(1)}, f32[512,512]{1,0:T(8,128)}) fusion(f32[512]{0:T(512)S(1)} %fusion.48, pred[512]{0:T(512)(128)(4,1)S(1)} %iota_compare_fusion.3), kind=kLoop, calls=%fused_computation.37 | loop fusion | flops 3932160 | bytes 2099712 | tf_op jit(solution)/shard_map/jit(_where)/select_n | solution.py:26
  31.7 35.9 %all-to-all-done = bf16[8,2,65536]{2,1,0:T(2,128)(2,1)} async-done(((bf16[8,2,65536]{2,1,0:T(2,128)(2,1)}), bf16[8,2,65536]{2,1,0:T(2,128)(2,1)}, u32[]{:S(2)}, u32[]{:S(2)}) %all-to-all-start) | async-done | bytes 2097184 | tf_op jit(solution)/shard_map/all_to_all | solution.py:114
  67.6 2.2 %reshape.211 = bf16[16,65536]{1,0:T(8,128)(2,1)S(1)} reshape(bf16[8,2,65536]{2,1,0:T(2,128)(2,1)} %all-to-all-done) | data formatting | bytes 4194304 | tf_op jit(solution)/shard_map/reshape | solution.py:116
  69.8 3.3 %gather_fusion = bf16[16,65536]{1,0:T(8,128)(2,1)} fusion(bf16[16,65536]{1,0:T(8,128)(2,1)S(1)} %reshape.211, s32[1024]{0:T(1024)S(1)} %pad_clamp_fusion), kind=kCustom, calls=%fused_computation | custom fusion | bytes 4194368 | tf_op jit(solution)/shard_map/jit(_take)/gather | solution.py:115
  73.1 2.3 %copy.30 = bf16[2,8,128,512]{3,2,1,0:T(8,128)(2,1)S(1)} copy(bf16[2,8,128,512]{3,1,2,0:T(8,128)(2,1)} %bitcast.50) | data formatting | bytes 4194304
  75.4 0.0 copy-start
  75.4 0.3 bitcast_select_fusion
  75.8 0.9 copy-done
  76.6 2.3 %fusion.12 = f32[16,128,1024]{2,1,0:T(8,128)S(1)} fusion(bf16[16,128,512]{2,1,0:T(8,128)(2,1)S(1)} %bitcast_select_fusion, f32[512,512]{1,0:T(8,128)S(1)} %get-tuple-element.15, f32[512,512]{1,0:T(8,128)S(1)} %copy-done), kind=kOutput, calls=%fused_computation.32 | convolution fusion | flops 2149580800 | bytes 12582912 | tf_op jit(solution)/shard_map/bcst,tk->bcsk/dot_general | solution.py:46
  79.0 2.5 %convolution_add_fusion = f32[16,128,1024]{2,1,0:T(8,128)S(1)} fusion(f32[16,128,1024]{2,1,0:T(8,128)S(1)} %fusion.12, bf16[16,128,512]{2,1,0:T(8,128)(2,1)S(1)} %bitcast_select_fusion, f32[512,512]{1,0:T(8,128)S(1)} %get-tuple-element.15, f32[512,512]{1,0:T(8,128)S(1)} %copy-done), kind=kOutput, calls=%fused_computation.8 | convolution fusion | flops 2152202240 | bytes 20971520 | tf_op jit(solution)/shard_map/bcst,tk->bcsk/dot_general | solution.py:47
  81.5 1.7 %slice_bitcast_fusion.1 = (f32[8,128,1,1024]{3,1,0,2:T(8,128)S(1)}, f32[8,128,1,1024]{3,1,0,2:T(8,128)S(1)}) fusion(f32[8,2,128,1,1024]{4,2,1,0,3:T(8,128)S(1)} %bitcast.49), kind=kLoop, calls=%fused_computation.3 | loop fusion | bytes 16777216 | tf_op jit(solution)/shard_map/squeeze | solution.py:120
  83.2 0.0 copy-start.1
  83.2 0.0 copy-start.2
  83.2 1.1 multiply_add_fusion.1
  84.3 0.0 copy-done.1
  84.3 0.2 copy-done.2
  84.6 6.7 %fusion.6 = f32[8,400,128]{2,1,0:T(8,128)} fusion(f32[8,128,1,512]{3,1,0,2:T(8,128)S(1)} %get-tuple-element.10, f32[8,128,1,512]{3,1,0,2:T(8,128)S(1)} %get-tuple-element.9, f32[512,400]{0,1:T(8,128)S(1)} %copy-done.2, f32[512,400]{0,1:T(8,128)S(1)} %copy-done.1), kind=kOutput, calls=%fused_computation.21 | convolution fusion | flops 5034622976 | bytes 7471104 | tf_op jit(solution)/shard_map/pck,kl->plc/dot_general | solution.py:62
  91.2 0.0 reduce-scatter.2.cloned.1.call-update
  91.3 28.7 %reduce-scatter.2.cloned.1.call-done = f32[4,400,128]{2,1,0:T(8,128)} async-done(((f32[8,400,128]{2,1,0:T(8,128)}), f32[4,400,128]{2,1,0:T(8,128)}) %reduce-scatter.2.cloned.1.call-update) | async-done | bytes 819216 | tf_op jit(solution)/shard_map/reduce_scatter | solution.py:123
  119.9 2.1 %broadcast_multiply_fusion = f32[4,400,128]{2,1,0:T(8,128)} fusion(f32[4,400,128]{2,1,0:T(8,128)} %reduce-scatter.2.cloned.1.call-done), kind=kLoop, calls=%fused_computation.55 | loop fusion | flops 204800 | bytes 1638400 | tf_op jit(solution)/shard_map/mul | solution.py:124
  (13 shorter events, 0.1 us)
Async XLA Ops:
  16.5 51.2 %all-to-all-start = ((bf16[8,2,65536]{2,1,0:T(2,128)(2,1)}), bf16[8,2,65536]{2,1,0:T(2,128)(2,1)}, u32[]{:S(2)}, u32[]{:S(2)}) async-start(bf16[8,2,65536]{2,1,0:T(2,128)(2,1)} %copy.25), calls=%async_computation | async-start | bytes 4194304 | tf_op jit(solution)/shard_map/all_to_all | solution.py:114
  22.1 97.8 %reduce-scatter.2.cloned.1.call-start = ((), (), s32[]{:S(2)}) async-start(), calls=%async_computation.2 | async-start | bytes 2457600 | tf_op jit(solution)/shard_map/reduce_scatter | solution.py:123
  75.4 1.2 copy-start
  83.2 1.2 copy-start.1
  83.2 1.4 %copy-start.2 = (f32[512,400]{0,1:T(8,128)S(1)}, f32[512,400]{0,1:T(8,128)}, u32[]{:S(2)}) copy-start(f32[512,400]{0,1:T(8,128)} %get-tuple-element.14) | copy-start | bytes 2457604
Sparse Core Ops, SparseCore 0:
  91.4 28.4 reduce-scatter.1
where the time goes:
time: 131 us; the launch traced here: 129 us
  waiting for transfers between devices  64.6 us (49%)
  local copies, waits for them, and re-layouts  16.5 us (13%)
  other arithmetic  14.5 us (11%)
  matrix products  14.1 us (11%)
  between operations  13.6 us (10%)
  starting transfers between devices  5.64 us (4%)
    all_to_all x1, waiting for transfers between devices, shards(): lax.all_to_all(outgoing, 'pair', split_axis=0, concat_axis=0, tiled=True)  35.9 us
    reduce_scatter x1, waiting for transfers between devices, shards(): stacked = lax.psum_scatter(lag_part, 'seg', scatter_dimension=0, tiled=True)  28.7 us
    dot_general x1, matrix products, to_lags(): jnp.einsum('pck,kl->plc', cross, inverse, precision=lax.Precision.HIGHEST)  6.69 us
    all_to_all x1, starting transfers between devices, shards(): lax.all_to_all(outgoing, 'pair', split_axis=0, concat_axis=0, tiled=True)  5.64 us
    select_n x1, other arithmetic, make_tables(): sine = jnp.where(first_bin[None, :], alternate[:, None], jnp.sin(angle))  4.92 us
    div x1, other arithmetic, make_tables(): upper = weight * jnp.cos(back_angle) / length  4.56 us
    unnamed x8, local copies, waits for them, and re-layouts  4.19 us
    convert_element_type x1, local copies, waits for them, and re-layouts, shards(): outgoing = jnp.einsum('drl,lx->drx', select.astype(jnp.bfloat16), payload...  3.46 us
  transfers between devices with their start and end apart: 2, of which 2 were waited for; matrix products, arithmetic and copies ran while one was open for 7% of the time, Pallas kernels for 0%

commit v1 on v0

--- a/solution.py
+++ b/solution.py
@@ -1,8 +1,12 @@
+import functools
 import math
 
 import jax
 import jax.numpy as jnp
+import numpy as np
 from jax import lax
+from jax.experimental import pallas as pl
+from jax.experimental.pallas import tpu as pltpu
 from jax.sharding import PartitionSpec as P
 
 CHB = 128
@@ -124,7 +128,228 @@
     return stacked * scale
 
 
+N = 768
+BINS = N // 2
+MESH = pl.DeviceIdType.MESH
+
+
+def lag_tables(scale):
+    freq = (2 * np.arange(BINS) + 1).astype(np.int64)
+    times = np.arange(WIN).astype(np.int64)
+    angle = (times[:, None] * freq[None, :] % (2 * N)) * (math.pi / N)
+    forward = np.concatenate([np.cos(angle), -np.sin(angle)], axis=1)
+    shifts = np.arange(LAGS).astype(np.int64) - MAXLAG
+    back = (freq[:, None] * shifts[None, :] % (2 * N)) * (math.pi / N)
+    inverse = np.concatenate([np.cos(back), -np.sin(back)], axis=0) * (2.0 * scale / N)
+    return forward.astype(jnp.bfloat16), inverse.astype(jnp.bfloat16)
+
+
+def exchange_kernel(
+    pair_count, seg_count, blk_dev, pairs_out, ch,
+    x_hbm, slot_ref, pairs_ref, f_hbm, w_hbm, recv2,
+    xv, yv, fv, wv, send1, recv1, spec, cross, send2,
+    local_sems, ss1, rs1, ss2, rs2,
+):
+    n = pair_count * seg_count
+    me = lax.axis_index("pair") * seg_count + lax.axis_index("seg")
+    rows = blk_dev * ch
+
+    def where(d):
+        return {"pair": d // seg_count, "seg": d % seg_count}
+
+    get_x = pltpu.make_async_copy(x_hbm, xv, local_sems.at[0])
+    get_f = pltpu.make_async_copy(f_hbm, fv, local_sems.at[1])
+    get_w = pltpu.make_async_copy(w_hbm, wv, local_sems.at[2])
+    get_x.start()
+    get_f.start()
+    get_w.start()
+
+    barrier = pltpu.get_barrier_semaphore()
+
+    def greet(i, carry):
+        pl.semaphore_signal(
+            barrier, inc=1, device_id=where((me + 1 + i) % n), device_id_type=MESH
+        )
+        return carry
+
+    lax.fori_loop(0, n - 1, greet, 0)
+
+    ti = lax.broadcasted_iota(jnp.int32, (WIN, WIN), 0)
+    tj = lax.broadcasted_iota(jnp.int32, (WIN, WIN), 1)
+    band = jnp.where(jnp.abs(ti - tj) <= HALF, 1.0, 0.0).astype(jnp.bfloat16)
+    t = lax.broadcasted_iota(jnp.int32, (1, WIN), 1)
+    count = (jnp.minimum(t + HALF, WIN - 1) - jnp.maximum(t - HALF, 0) + 1).astype(jnp.float32)
+    get_x.wait()
+    x = xv[...]
+    mag = jnp.abs(x)
+    high = mag.astype(jnp.bfloat16)
+    low = (mag - high.astype(jnp.float32)).astype(jnp.bfloat16)
+    sums = jnp.dot(high, band, preferred_element_type=jnp.float32) + jnp.dot(
+        low, band, preferred_element_type=jnp.float32
+    )
+    yv[...] = x / (sums / count + EPS)
+
+    def regroup(d, carry):
+        parts = [
+            yv[pl.ds(pl.multiple_of(b * CHB + d * ch, ch), ch), :] for b in range(blk_dev)
+        ]
+        send1[d] = jnp.concatenate(parts, axis=0).astype(jnp.bfloat16)
+        return carry
+
+    lax.fori_loop(0, n, regroup, 0)
+    pl.semaphore_wait(barrier, n - 1)
+
+    def copy1(d, src):
+        return pltpu.make_async_remote_copy(
+            src_ref=send1.at[d], dst_ref=recv1.at[src], send_sem=ss1.at[d], recv_sem=rs1.at[src],
+            device_id=where(d), device_id_type=MESH,
+        )
+
+    def copy2(d, src):
+        return pltpu.make_async_remote_copy(
+            src_ref=send2.at[d], dst_ref=recv2.at[src], send_sem=ss2.at[d], recv_sem=rs2.at[src],
+            device_id=where(d), device_id_type=MESH,
+        )
+
+    def start1(i, carry):
+        copy1((me + n // 2 + i + (i >= n // 2).astype(jnp.int32)) % n, me).start()
+        return carry
+
+    lax.fori_loop(0, n - 1, start1, 0)
+    recv1[me] = send1[me]
+
+    def arrive1(i, carry):
+        src = (me + 1 + i) % n
+        copy1(src, src).wait_recv()
+        return carry
+
+    get_f.wait()
+    lax.fori_loop(0, n - 1, arrive1, 0)
+
+    got = recv1[...].reshape(n * rows, WIN)
+    full = jnp.dot(got, fv[...], preferred_element_type=jnp.float32)
+    for p in range(pair_count):
+        for s in range(seg_count):
+            for b in range(blk_dev):
+                at = (p * seg_count + s) * rows + b * ch
+                spec[p * blk_dev + b, s] = full[at : at + ch]
+    get_w.wait()
+
+    group = n // 4
+    first = me // group
+
+    def one_pair(q):
+        u = spec[slot_ref[pairs_ref[q, 0]]]
+        v = spec[slot_ref[pairs_ref[q, 1]]]
+        ur, ui, vr, vi = u[..., :BINS], u[..., BINS:], v[..., :BINS], v[..., BINS:]
+        re = jnp.sum(ur * vr + ui * vi, axis=0)
+        im = jnp.sum(ur * vi - ui * vr, axis=0)
+        return jnp.concatenate([re, im], axis=1)
+
+    step = 16 // ch
+
+    def chunk(k, carry):
+        c = (first + 2 + k) % 4
+        for j in range(group * pairs_out // step):
+            q = c * (group * pairs_out) + j * step
+            cross[j * 16 : (j + 1) * 16, :] = jnp.concatenate(
+                [one_pair(q + i) for i in range(step)], axis=0
+            ).astype(jnp.bfloat16)
+        lags = jnp.dot(cross[...], wv[...], preferred_element_type=jnp.float32)
+        send2[pl.ds(c * group, group)] = lags.astype(jnp.bfloat16).reshape(
+            group, pairs_out * ch, LAGS
+        )
+        for g in range(group):
+            d = c * group + g
+
+            @pl.when(d != me)
+            def _():
+                copy2(d, me).start()
+
+        return carry
+
+    lax.fori_loop(0, 4, chunk, 0)
+    recv2[me] = send2[me]
+
+    def arrive2(i, carry):
+        src = (me + 1 + i) % n
+        copy2(src, src).wait_recv()
+        copy1(src, src).wait_send()
+        copy2(src, src).wait_send()
+        return carry
+
+    lax.fori_loop(0, n - 1, arrive2, 0)
+
+
+def layout_kernel(n, ch, r_ref, o_ref):
+    for j in range(o_ref.shape[0]):
+        part = r_ref[...].astype(jnp.float32)[:, j * ch : (j + 1) * ch, :]
+        o_ref[j] = part.reshape(n * ch, LAGS).T
+
+
+def channel_shards(strain, block_slot, pair_blocks):
+    pair_count = lax.axis_size("pair")
+    seg_count = lax.axis_size("seg")
+    n = pair_count * seg_count
+    blk_dev = strain.shape[0] // CHB
+    nblk = block_slot.shape[0]
+    pairs_out = pair_blocks.shape[0] // n
+    ch = CHB // n
+    rows = blk_dev * ch
+    forward, inverse = lag_tables(1.0 / math.sqrt(seg_count * WIN))
+    group = n // 4
+    any_spec = pl.BlockSpec(memory_space=pl.ANY)
+    smem = pl.BlockSpec(memory_space=pltpu.SMEM)
+    parts = pl.pallas_call(
+        functools.partial(exchange_kernel, pair_count, seg_count, blk_dev, pairs_out, ch),
+        out_shape=jax.ShapeDtypeStruct((n, pairs_out * ch, LAGS), jnp.bfloat16),
+        in_specs=[any_spec, smem, smem, any_spec, any_spec],
+        out_specs=pl.BlockSpec(memory_space=pltpu.VMEM),
+        scratch_shapes=[
+            pltpu.VMEM((blk_dev * CHB, WIN), jnp.float32),
+            pltpu.VMEM((blk_dev * CHB, WIN), jnp.float32),
+            pltpu.VMEM(forward.shape, jnp.bfloat16),
+            pltpu.VMEM(inverse.shape, jnp.bfloat16),
+            pltpu.VMEM((n, rows, WIN), jnp.bfloat16),
+            pltpu.VMEM((n, rows, WIN), jnp.bfloat16),
+            pltpu.VMEM((nblk, seg_count, ch, N), jnp.float32),
+            pltpu.VMEM((group * pairs_out * ch, N), jnp.bfloat16),
+            pltpu.VMEM((n, pairs_out * ch, LAGS), jnp.bfloat16),
+            pltpu.SemaphoreType.DMA((3,)),
+            pltpu.SemaphoreType.DMA((n,)),
+            pltpu.SemaphoreType.DMA((n,)),
+            pltpu.SemaphoreType.DMA((n,)),
+            pltpu.SemaphoreType.DMA((n,)),
+        ],
+        compiler_params=pltpu.CompilerParams(
+            collective_id=0, has_side_effects=True, vmem_limit_bytes=32 * 1024 * 1024
+        ),
+        name="exchange",
+    )(strain, block_slot, pair_blocks, jnp.asarray(forward), jnp.asarray(inverse))
+    return pl.pallas_call(
+        functools.partial(layout_kernel, n, ch),
+        out_shape=jax.ShapeDtypeStruct((pairs_out, LAGS, CHB), jnp.float32),
+        in_specs=[pl.BlockSpec(memory_space=pltpu.VMEM)],
+        out_specs=pl.BlockSpec(memory_space=pltpu.VMEM),
+        compiler_params=pltpu.CompilerParams(vmem_limit_bytes=32 * 1024 * 1024),
+        name="layout",
+    )(parts)
+
+
+def fits_channels(mesh):
+    n = mesh.shape["pair"] * mesh.shape["seg"]
+    return mesh.shape["lag"] == 1 and n % 4 == 0 and CHB % n == 0 and CHB // n in (8, 16)
+
+
 def solution(mesh):
     in_specs = (P(("grp", "pair"), "seg"), P("grp"), P("grp", None))
     out_specs = P(("grp", "pair", "seg"), "lag", None)
-    return jax.shard_map(shards, mesh=mesh, in_specs=in_specs, out_specs=out_specs, check_vma=False)
+
+    def run(strain, block_slot, pair_blocks):
+        one_segment = strain.shape[1] == WIN * mesh.shape["seg"]
+        body = channel_shards if fits_channels(mesh) and one_segment else shards
+        return jax.shard_map(
+            body, mesh=mesh, in_specs=in_specs, out_specs=out_specs, check_vma=False
+        )(strain, block_slot, pair_blocks)
+
+    return run

time: 131 us -> 32.6 us (0.25); the launches traced: 129 us -> 32.3 us
  waiting for transfers between devices: 64.6 us -> 0 us
  Pallas kernels: 0 us -> 28.2 us
  other arithmetic: 14.5 us -> 0 us
  matrix products: 14.1 us -> 0 us
  between operations: 13.6 us -> 0.02 us
  local copies, waits for them, and re-layouts: 16.5 us -> 4.08 us
  starting transfers between devices: 5.64 us -> 0 us
    all_to_all x1 -> x0, waiting for transfers between devices: 35.9 us -> none  [shards(): lax.all_to_all(outgoing, 'pair', split_axis=0, concat_axis=0, tiled=True)]
    reduce_scatter x1 -> x0, waiting for transfers between devices: 28.7 us -> none  [shards(): stacked = lax.psum_scatter(lag_part, 'seg', scatter_dimension=0, tiled=True)]
    pallas_call x0 -> x2, Pallas kernels: none -> 28.2 us  [the longest x1 27.1 us: channel_shards(): pl.pallas_call(functools.partial(exchange_kernel, pair_count, seg_count,...]
    dot_general x6 -> x0, matrix products: 14.1 us -> none  [the longest x1 6.69 us: to_lags(): jnp.einsum('pck,kl->plc', cross, inverse, precision=lax.Precision.HIGHEST)]
    all_to_all x1 -> x0, starting transfers between devices: 5.64 us -> none  [shards(): lax.all_to_all(outgoing, 'pair', split_axis=0, concat_axis=0, tiled=True)]
    select_n x5 -> x0, other arithmetic: 5.28 us -> none  [the longest x1 4.92 us: make_tables(): sine = jnp.where(first_bin[None, :], alternate[:, None], jnp.sin(angle))]
    div x2 -> x0, other arithmetic: 4.58 us -> none  [the longest x1 4.56 us: make_tables(): upper = weight * jnp.cos(back_angle) / length]
    reshape x3 -> x0, local copies, waits for them, and re-layouts: 3.65 us -> none  [the longest x1 2.24 us: shards(): incoming.reshape(pair_count * capacity, CHB * seg_dev * WIN)]
  transfers between devices with their start and end apart: 2 -> 0, of which waited for: 2 -> 0; matrix products, arithmetic and copies ran while one was open for 7% -> 0% of each run, Pallas kernels for 0% -> 0%
where the time goes in v1:
time: 32.6 us; the launch traced here: 32.3 us
  Pallas kernels  28.2 us (87%)
  local copies, waits for them, and re-layouts  4.08 us (13%)
    pallas_call x1, Pallas kernels, channel_shards(): pl.pallas_call(functools.partial(exchange_kernel, pair_count, seg_count,...  27.1 us
    unnamed x9, local copies, waits for them, and re-layouts  4.08 us
    pallas_call x1, Pallas kernels, channel_shards(): pl.pallas_call(functools.partial(layout_kernel, n, ch), out_shape=jax.Sha...  1.1 us

profile of v1, /device:TPU:9, one launch (start us, length us, event | category | flops | bytes accessed | tf_op | source)
XLA Modules:
  0.0 32.3 jit_solution(2289801263678193765)
XLA Ops:
  0.0 0.0 copy-start.3
  0.0 0.8 %copy.6.pairs_ref = s32[64,2]{1,0:T(8,128)S(1)} copy(s32[64,2]{0,1:T(2,128)} %param.7) | data formatting | bytes 1024 | tf_op args[2]
  0.8 0.0 copy-done.3
  0.8 0.0 copy-start
  0.8 1.1 %copy-done = bf16[768,400]{1,0:T(8,128)(2,1)S(1)} copy-done((bf16[768,400]{1,0:T(8,128)(2,1)S(1)}, bf16[768,400]{1,0:T(8,128)(2,1)}, u32[]{:S(2)}) %copy-start) | copy-done | bytes 614424
  1.9 0.0 copy-start.1
  1.9 1.1 %copy-done.1 = bf16[512,768]{1,0:T(8,128)(2,1)S(1)} copy-done((bf16[512,768]{1,0:T(8,128)(2,1)S(1)}, bf16[512,768]{1,0:T(8,128)(2,1)}, u32[]{:S(2)}) %copy-start.1) | copy-done | bytes 786456
  3.1 0.0 copy-start.2
  3.1 1.0 %copy-done.2 = f32[256,512]{1,0:T(8,128)S(1)} copy-done((f32[256,512]{1,0:T(8,128)S(1)}, f32[256,512]{1,0:T(8,128)}, u32[]{:S(2)}) %copy-start.2) | copy-done | bytes 524312
  4.1 27.1 %exchange.1.r_ref = bf16[16,32,400]{2,1,0:T(8,128)(2,1)S(1)} custom-call(f32[256,512]{1,0:T(8,128)S(1)} %copy-done.2, s32[16]{0:T(128)S(1)} %copy-done.3, s32[64,2]{1,0:T(8,128)S(1)} %copy.6.pairs_ref, bf16[512,768]{1,0:T(8,128)(2,1)S(1)} %copy-done.1, bf16[768,400]{1,0:T(8,128)(2,1)S(1)} %copy-done), custom_call_target="tpu_custom_call" | custom-call | tf_op jit(solution)/shard_map/exchange/pallas_call | solution.py:303
  31.2 1.1 %layout.1 = f32[4,400,128]{2,1,0:T(8,128)} custom-call(bf16[16,32,400]{2,1,0:T(8,128)(2,1)S(1)} %exchange.1.r_ref), custom_call_target="tpu_custom_call" | custom-call | tf_op jit(solution)/shard_map/layout/pallas_call | solution.py:329
Async XLA Ops:
  0.0 0.8 %copy-start.3 = (s32[16]{0:T(128)S(1)}, s32[16]{0:T(128)}, u32[]{:S(2)}) copy-start(s32[16]{0:T(128)} %slot_ref.1) | copy-start | bytes 196
  0.8 1.1 %copy-start = (bf16[768,400]{1,0:T(8,128)(2,1)S(1)}, bf16[768,400]{1,0:T(8,128)(2,1)}, u32[]{:S(2)}) copy-start(bf16[768,400]{1,0:T(8,128)(2,1)} %constant.5.clone.w_hbm) | copy-start | bytes 1843204
  1.9 1.1 %copy-start.1 = (bf16[512,768]{1,0:T(8,128)(2,1)S(1)}, bf16[512,768]{1,0:T(8,128)(2,1)}, u32[]{:S(2)}) copy-start(bf16[512,768]{1,0:T(8,128)(2,1)} %constant.4.clone.f_hbm) | copy-start | bytes 2359300
  3.1 1.0 %copy-start.2 = (f32[256,512]{1,0:T(8,128)S(1)}, f32[256,512]{1,0:T(8,128)}, u32[]{:S(2)}) copy-start(f32[256,512]{1,0:T(8,128)} %x_hbm.1) | copy-start | bytes 1572868

commit v2 on v1

--- a/solution.py
+++ b/solution.py
@@ -130,6 +130,9 @@
 
 N = 768
 BINS = N // 2
+LANES = 128
+BULK = LAGS // LANES * LANES
+TAIL = LAGS - BULK
 MESH = pl.DeviceIdType.MESH
 
 
@@ -141,28 +144,35 @@
     shifts = np.arange(LAGS).astype(np.int64) - MAXLAG
     back = (freq[:, None] * shifts[None, :] % (2 * N)) * (math.pi / N)
     inverse = np.concatenate([np.cos(back), -np.sin(back)], axis=0) * (2.0 * scale / N)
+    tail = inverse[:, BULK:]
+    blank = np.zeros((N, LANES - 2 * TAIL))
+    inverse = np.concatenate([inverse, tail, blank], axis=1)
     return forward.astype(jnp.bfloat16), inverse.astype(jnp.bfloat16)
 
 
 def exchange_kernel(
     pair_count, seg_count, blk_dev, pairs_out, ch,
-    x_hbm, slot_ref, pairs_ref, f_hbm, w_hbm, recv2,
-    xv, yv, fv, wv, send1, recv1, spec, cross, send2,
+    x_hbm, slot_hbm, pairs_hbm, f_hbm, w_hbm, recv2,
+    xv, slot_ref, pairs_ref, fv, wv, band, send1, recv1, spec, cross, send2,
     local_sems, ss1, rs1, ss2, rs2,
 ):
     n = pair_count * seg_count
     me = lax.axis_index("pair") * seg_count + lax.axis_index("seg")
     rows = blk_dev * ch
+    group = n // 4
+    first = me // group
 
     def where(d):
         return {"pair": d // seg_count, "seg": d % seg_count}
 
-    get_x = pltpu.make_async_copy(x_hbm, xv, local_sems.at[0])
-    get_f = pltpu.make_async_copy(f_hbm, fv, local_sems.at[1])
-    get_w = pltpu.make_async_copy(w_hbm, wv, local_sems.at[2])
-    get_x.start()
-    get_f.start()
-    get_w.start()
+    gets = [
+        pltpu.make_async_copy(src, dst, local_sems.at[i])
+        for i, (src, dst) in enumerate(
+            [(x_hbm, xv), (f_hbm, fv), (w_hbm, wv), (slot_hbm, slot_ref), (pairs_hbm, pairs_ref)]
+        )
+    ]
+    for get in gets:
+        get.start()
 
     barrier = pltpu.get_barrier_semaphore()
 
@@ -173,31 +183,6 @@
         return carry
 
     lax.fori_loop(0, n - 1, greet, 0)
-
-    ti = lax.broadcasted_iota(jnp.int32, (WIN, WIN), 0)
-    tj = lax.broadcasted_iota(jnp.int32, (WIN, WIN), 1)
-    band = jnp.where(jnp.abs(ti - tj) <= HALF, 1.0, 0.0).astype(jnp.bfloat16)
-    t = lax.broadcasted_iota(jnp.int32, (1, WIN), 1)
-    count = (jnp.minimum(t + HALF, WIN - 1) - jnp.maximum(t - HALF, 0) + 1).astype(jnp.float32)
-    get_x.wait()
-    x = xv[...]
-    mag = jnp.abs(x)
-    high = mag.astype(jnp.bfloat16)
-    low = (mag - high.astype(jnp.float32)).astype(jnp.bfloat16)
-    sums = jnp.dot(high, band, preferred_element_type=jnp.float32) + jnp.dot(
-        low, band, preferred_element_type=jnp.float32
-    )
-    yv[...] = x / (sums / count + EPS)
-
-    def regroup(d, carry):
-        parts = [
-            yv[pl.ds(pl.multiple_of(b * CHB + d * ch, ch), ch), :] for b in range(blk_dev)
-        ]
-        send1[d] = jnp.concatenate(parts, axis=0).astype(jnp.bfloat16)
-        return carry
-
-    lax.fori_loop(0, n, regroup, 0)
-    pl.semaphore_wait(barrier, n - 1)
 
     def copy1(d, src):
         return pltpu.make_async_remote_copy(
@@ -211,56 +196,97 @@
             device_id=where(d), device_id_type=MESH,
         )
 
-    def start1(i, carry):
-        copy1((me + n // 2 + i + (i >= n // 2).astype(jnp.int32)) % n, me).start()
-        return carry
-
-    lax.fori_loop(0, n - 1, start1, 0)
+    def quarter(k):
+        high = (first // 2 + jnp.where(k < 2, 1, 0)) % 2
+        low = (first + jnp.where((k == 1) | (k == 2), 1, 0)) % 2
+        return 2 * high + low
+
+    ti = lax.broadcasted_iota(jnp.int32, (WIN, WIN), 0)
+    tj = lax.broadcasted_iota(jnp.int32, (WIN, WIN), 1)
+    band[...] = jnp.where(jnp.abs(ti - tj) <= HALF, 1.0, 0.0).astype(jnp.bfloat16)
+    t = lax.broadcasted_iota(jnp.int32, (1, WIN), 1)
+    count = (jnp.minimum(t + HALF, WIN - 1) - jnp.maximum(t - HALF, 0) + 1).astype(jnp.float32)
+    gets[0].wait()
+
+    for k in range(4):
+        c = quarter(k)
+        span = group * ch
+        x = jnp.concatenate(
+            [xv[pl.ds(pl.multiple_of(b * CHB + c * span, span), span), :] for b in range(blk_dev)],
+            axis=0,
+        )
+        mag = jnp.abs(x)
+        high = mag.astype(jnp.bfloat16)
+        low = (mag - high.astype(jnp.float32)).astype(jnp.bfloat16)
+        sums = jnp.dot(high, band[...], preferred_element_type=jnp.float32) + jnp.dot(
+            low, band[...], preferred_element_type=jnp.float32
+        )
+        y = x / (sums / count + EPS)
+        for g in range(group):
+            part = [y[b * span + g * ch : b * span + (g + 1) * ch] for b in range(blk_dev)]
+            send1[c * group + g] = jnp.concatenate(part, axis=0).astype(jnp.bfloat16)
+        if k == 0:
+            pl.semaphore_wait(barrier, n - 1)
+        for g in range(group):
+            d = c * group + g
+
+            @pl.when(d != me)
+            def _():
+                copy1(d, me).start()
+
     recv1[me] = send1[me]
-
-    def arrive1(i, carry):
-        src = (me + 1 + i) % n
-        copy1(src, src).wait_recv()
-        return carry
-
-    get_f.wait()
-    lax.fori_loop(0, n - 1, arrive1, 0)
-
-    got = recv1[...].reshape(n * rows, WIN)
-    full = jnp.dot(got, fv[...], preferred_element_type=jnp.float32)
-    for p in range(pair_count):
-        for s in range(seg_count):
+    gets[1].wait()
+
+    for k in (3, 2, 1, 0):
+        c = quarter(k)
+        for g in range(group):
+            src = c * group + g
+
+            @pl.when(src != me)
+            def _():
+                copy1(src, src).wait_recv()
+
+        got = recv1[pl.ds(c * group, group)].reshape(group * rows, WIN)
+        full = jnp.dot(got, fv[...], preferred_element_type=jnp.float32)
+        for g in range(group):
+            p = c * (group // seg_count) + g // seg_count
             for b in range(blk_dev):
-                at = (p * seg_count + s) * rows + b * ch
-                spec[p * blk_dev + b, s] = full[at : at + ch]
-    get_w.wait()
-
-    group = n // 4
-    first = me // group
+                at = g * rows + b * ch
+                spec[p * blk_dev + b, g % seg_count] = full[at : at + ch]
+    for get in gets[2:]:
+        get.wait()
 
     def one_pair(q):
-        u = spec[slot_ref[pairs_ref[q, 0]]]
-        v = spec[slot_ref[pairs_ref[q, 1]]]
+        u = spec[slot_ref[pairs_ref[0, q]]]
+        v = spec[slot_ref[pairs_ref[1, q]]]
         ur, ui, vr, vi = u[..., :BINS], u[..., BINS:], v[..., :BINS], v[..., BINS:]
         re = jnp.sum(ur * vr + ui * vi, axis=0)
         im = jnp.sum(ur * vi - ui * vr, axis=0)
         return jnp.concatenate([re, im], axis=1)
 
     step = 16 // ch
+    size = pairs_out * ch
 
     def chunk(k, carry):
-        c = (first + 2 + k) % 4
+        c = quarter(k)
         for j in range(group * pairs_out // step):
             q = c * (group * pairs_out) + j * step
             cross[j * 16 : (j + 1) * 16, :] = jnp.concatenate(
                 [one_pair(q + i) for i in range(step)], axis=0
             ).astype(jnp.bfloat16)
         lags = jnp.dot(cross[...], wv[...], preferred_element_type=jnp.float32)
-        send2[pl.ds(c * group, group)] = lags.astype(jnp.bfloat16).reshape(
-            group, pairs_out * ch, LAGS
-        )
         for g in range(group):
             d = c * group + g
+            mine = lags[g * size : (g + 1) * size]
+            for m in range(BULK // LANES):
+                send2[d, m * size : (m + 1) * size, :] = mine[
+                    :, m * LANES : (m + 1) * LANES
+                ].astype(jnp.bfloat16)
+            rest = mine[:, BULK:]
+            lane = lax.broadcasted_iota(jnp.int32, (size // 2, LANES), 1)
+            send2[d, BULK // LANES * size :, :] = jnp.where(
+                lane < TAIL, rest[: size // 2], rest[size // 2 :]
+            ).astype(jnp.bfloat16)
 
             @pl.when(d != me)
             def _():
@@ -281,10 +307,24 @@
     lax.fori_loop(0, n - 1, arrive2, 0)
 
 
-def layout_kernel(n, ch, r_ref, o_ref):
-    for j in range(o_ref.shape[0]):
-        part = r_ref[...].astype(jnp.float32)[:, j * ch : (j + 1) * ch, :]
-        o_ref[j] = part.reshape(n * ch, LAGS).T
+def layout_kernel(n, ch, r_ref, o_hbm, ov, sems):
+    pairs_out = ov.shape[0]
+    size = pairs_out * ch
+    tiles = BULK // LANES
+
+    def turned(row):
+        return r_ref[:, row : row + ch, :].astype(jnp.float32).reshape(n * ch, LANES).T
+
+    half = pairs_out // 2
+    for j in range(half):
+        rest = turned(tiles * size + j * ch)
+        for i, p in enumerate((j, j + half)):
+            for m in range(tiles):
+                ov[p, m * LANES : (m + 1) * LANES, :] = turned(m * size + p * ch)
+            ov[p, BULK:, :] = rest[i * TAIL : (i + 1) * TAIL]
+            pltpu.make_async_copy(ov.at[p], o_hbm.at[p], sems.at[p]).start()
+    for p in range(pairs_out):
+        pltpu.make_async_copy(ov.at[p], o_hbm.at[p], sems.at[p]).wait()
 
 
 def channel_shards(strain, block_slot, pair_blocks):
@@ -296,41 +336,47 @@
     pairs_out = pair_blocks.shape[0] // n
     ch = CHB // n
     rows = blk_dev * ch
+    message = pairs_out * ch // 2 * (2 * BULK // LANES + 1)
     forward, inverse = lag_tables(1.0 / math.sqrt(seg_count * WIN))
     group = n // 4
     any_spec = pl.BlockSpec(memory_space=pl.ANY)
-    smem = pl.BlockSpec(memory_space=pltpu.SMEM)
     parts = pl.pallas_call(
         functools.partial(exchange_kernel, pair_count, seg_count, blk_dev, pairs_out, ch),
-        out_shape=jax.ShapeDtypeStruct((n, pairs_out * ch, LAGS), jnp.bfloat16),
-        in_specs=[any_spec, smem, smem, any_spec, any_spec],
+        out_shape=jax.ShapeDtypeStruct((n, message, LANES), jnp.bfloat16),
+        in_specs=[any_spec] * 5,
         out_specs=pl.BlockSpec(memory_space=pltpu.VMEM),
         scratch_shapes=[
             pltpu.VMEM((blk_dev * CHB, WIN), jnp.float32),
-            pltpu.VMEM((blk_dev * CHB, WIN), jnp.float32),
+            pltpu.SMEM((nblk,), jnp.int32),
+            pltpu.SMEM((2, pair_blocks.shape[0]), jnp.int32),
             pltpu.VMEM(forward.shape, jnp.bfloat16),
             pltpu.VMEM(inverse.shape, jnp.bfloat16),
+            pltpu.VMEM((WIN, WIN), jnp.bfloat16),
             pltpu.VMEM((n, rows, WIN), jnp.bfloat16),
             pltpu.VMEM((n, rows, WIN), jnp.bfloat16),
             pltpu.VMEM((nblk, seg_count, ch, N), jnp.float32),
             pltpu.VMEM((group * pairs_out * ch, N), jnp.bfloat16),
-            pltpu.VMEM((n, pairs_out * ch, LAGS), jnp.bfloat16),
-            pltpu.SemaphoreType.DMA((3,)),
+            pltpu.VMEM((n, message, LANES), jnp.bfloat16),
+            pltpu.SemaphoreType.DMA((5,)),
             pltpu.SemaphoreType.DMA((n,)),
             pltpu.SemaphoreType.DMA((n,)),
             pltpu.SemaphoreType.DMA((n,)),
             pltpu.SemaphoreType.DMA((n,)),
         ],
         compiler_params=pltpu.CompilerParams(
-            collective_id=0, has_side_effects=True, vmem_limit_bytes=32 * 1024 * 1024
+            collective_id=0, has_side_effects=True, vmem_limit_bytes=62 * 1024 * 1024
         ),
         name="exchange",
-    )(strain, block_slot, pair_blocks, jnp.asarray(forward), jnp.asarray(inverse))
+    )(strain, block_slot, pair_blocks.T, jnp.asarray(forward), jnp.asarray(inverse))
     return pl.pallas_call(
         functools.partial(layout_kernel, n, ch),
         out_shape=jax.ShapeDtypeStruct((pairs_out, LAGS, CHB), jnp.float32),
         in_specs=[pl.BlockSpec(memory_space=pltpu.VMEM)],
-        out_specs=pl.BlockSpec(memory_space=pltpu.VMEM),
+        out_specs=any_spec,
+        scratch_shapes=[
+            pltpu.VMEM((pairs_out, LAGS, CHB), jnp.float32),
+            pltpu.SemaphoreType.DMA((pairs_out,)),
+        ],
         compiler_params=pltpu.CompilerParams(vmem_limit_bytes=32 * 1024 * 1024),
         name="layout",
     )(parts)
@@ -338,7 +384,8 @@
 
 def fits_channels(mesh):
     n = mesh.shape["pair"] * mesh.shape["seg"]
-    return mesh.shape["lag"] == 1 and n % 4 == 0 and CHB % n == 0 and CHB // n in (8, 16)
+    whole = n % (4 * mesh.shape["seg"]) == 0 and CHB % n == 0
+    return mesh.shape["lag"] == 1 and whole and CHB // n in (8, 16)
 
 
 def solution(mesh):

time: 32.6 us -> 27.4 us (0.84)
  local copies, waits for them, and re-layouts: 4.08 us -> 1.01 us
  Pallas kernels: 28.2 us -> 26.2 us
    unnamed x9 -> x2, local copies, waits for them, and re-layouts: 4.08 us -> 1.01 us
    pallas_call x1, Pallas kernels: 27.1 us -> 25.1 us  [channel_shards(): pl.pallas_call(functools.partial(exchange_kernel, pair_count, seg_count,...]
where the time goes in v2:
time: 27.4 us; the launch traced here: 27.2 us
  Pallas kernels  26.2 us (96%)
  local copies, waits for them, and re-layouts  1.01 us (4%)
    pallas_call x1, Pallas kernels, channel_shards(): pl.pallas_call(functools.partial(exchange_kernel, pair_count, seg_count,...  25.1 us
    pallas_call x1, Pallas kernels, channel_shards(): pl.pallas_call(functools.partial(layout_kernel, n, ch), out_shape=jax.Sha...  1.05 us
    unnamed x2, local copies, waits for them, and re-layouts  1.01 us

profile of v2, /device:TPU:9, one launch (start us, length us, event | category | flops | bytes accessed | tf_op | source)
XLA Modules:
  0.0 27.2 jit_solution(4447991241336070786)
XLA Ops:
  0.0 25.1 %exchange.1.r_ref = bf16[16,112,128]{2,1,0:T(8,128)(2,1)} custom-call(f32[256,512]{1,0:T(8,128)} %x_hbm.1, s32[16]{0:T(128)} %slot_hbm.1, s32[2,64]{1,0:T(2,128)} %bitcast.1, bf16[512,768]{1,0:T(8,128)(2,1)} %constant.4.clone.f_hbm, bf16[768,512]{1,0:T(8,128)(2,1)} %constant.5.clone.w_hbm), custom_call_target="tpu_custom_call" | custom-call | tf_op jit(solution)/shard_map/exchange/pallas_call | solution.py:343
  25.1 0.0 copy-start
  25.2 1.0 %copy-done = bf16[16,112,128]{2,1,0:T(8,128)(2,1)S(1)} copy-done((bf16[16,112,128]{2,1,0:T(8,128)(2,1)S(1)}, bf16[16,112,128]{2,1,0:T(8,128)(2,1)}, u32[]{:S(2)}) %copy-start) | copy-done | bytes 458776
  26.2 1.1 %layout.1 = f32[4,400,128]{2,1,0:T(8,128)} custom-call(bf16[16,112,128]{2,1,0:T(8,128)(2,1)S(1)} %copy-done), custom_call_target="tpu_custom_call" | custom-call | tf_op jit(solution)/shard_map/layout/pallas_call | solution.py:371
Async XLA Ops:
  25.1 1.0 %copy-start = (bf16[16,112,128]{2,1,0:T(8,128)(2,1)S(1)}, bf16[16,112,128]{2,1,0:T(8,128)(2,1)}, u32[]{:S(2)}) copy-start(bf16[16,112,128]{2,1,0:T(8,128)(2,1)} %exchange.1.r_ref) | copy-start | bytes 1376260

commit v3 on v2

--- a/solution.py
+++ b/solution.py
@@ -160,7 +160,10 @@
     me = lax.axis_index("pair") * seg_count + lax.axis_index("seg")
     rows = blk_dev * ch
     group = n // 4
+    half = n // 2
     first = me // group
+    side, place = me // half, me % half
+    size = pairs_out * ch
 
     def where(d):
         return {"pair": d // seg_count, "seg": d % seg_count}
@@ -184,15 +187,17 @@
 
     lax.fori_loop(0, n - 1, greet, 0)
 
-    def copy1(d, src):
+    def copy1(r, d, src):
         return pltpu.make_async_remote_copy(
-            src_ref=send1.at[d], dst_ref=recv1.at[src], send_sem=ss1.at[d], recv_sem=rs1.at[src],
+            src_ref=send1.at[r * half + d % half], dst_ref=recv1.at[r * n + src],
+            send_sem=ss1.at[r * n + d], recv_sem=rs1.at[r * n + src],
             device_id=where(d), device_id_type=MESH,
         )
 
-    def copy2(d, src):
+    def copy2(r, d, src):
         return pltpu.make_async_remote_copy(
-            src_ref=send2.at[d], dst_ref=recv2.at[src], send_sem=ss2.at[d], recv_sem=rs2.at[src],
+            src_ref=send2.at[r * half + d % half], dst_ref=recv2.at[src % half * 2 + r],
+            send_sem=ss2.at[r * half + d % half], recv_sem=rs2.at[src % half * 2 + r],
             device_id=where(d), device_id_type=MESH,
         )
 
@@ -208,12 +213,10 @@
     count = (jnp.minimum(t + HALF, WIN - 1) - jnp.maximum(t - HALF, 0) + 1).astype(jnp.float32)
     gets[0].wait()
 
-    for k in range(4):
-        c = quarter(k)
-        span = group * ch
+    span = half * ch
+    for m in range(2):
         x = jnp.concatenate(
-            [xv[pl.ds(pl.multiple_of(b * CHB + c * span, span), span), :] for b in range(blk_dev)],
-            axis=0,
+            [xv[b * CHB + m * span : b * CHB + (m + 1) * span, :] for b in range(blk_dev)], axis=0
         )
         mag = jnp.abs(x)
         high = mag.astype(jnp.bfloat16)
@@ -223,37 +226,26 @@
         )
         y = x / (sums / count + EPS)
         for g in range(group):
-            part = [y[b * span + g * ch : b * span + (g + 1) * ch] for b in range(blk_dev)]
-            send1[c * group + g] = jnp.concatenate(part, axis=0).astype(jnp.bfloat16)
-        if k == 0:
-            pl.semaphore_wait(barrier, n - 1)
-        for g in range(group):
-            d = c * group + g
-
-            @pl.when(d != me)
-            def _():
-                copy1(d, me).start()
-
-    recv1[me] = send1[me]
-    gets[1].wait()
-
-    for k in (3, 2, 1, 0):
-        c = quarter(k)
-        for g in range(group):
-            src = c * group + g
-
-            @pl.when(src != me)
-            def _():
-                copy1(src, src).wait_recv()
-
-        got = recv1[pl.ds(c * group, group)].reshape(group * rows, WIN)
-        full = jnp.dot(got, fv[...], preferred_element_type=jnp.float32)
-        for g in range(group):
-            p = c * (group // seg_count) + g // seg_count
-            for b in range(blk_dev):
-                at = g * rows + b * ch
-                spec[p * blk_dev + b, g % seg_count] = full[at : at + ch]
-    for get in gets[2:]:
+            for r in range(2):
+                at = (2 * g + r) * ch
+                part = [y[b * span + at : b * span + at + ch] for b in range(blk_dev)]
+                send1[r * half + m * group + g] = jnp.concatenate(part, axis=0).astype(jnp.bfloat16)
+    pl.semaphore_wait(barrier, n - 1)
+
+    for r in range(2):
+
+        def across(i, carry):
+            copy1(r, (1 - side) * half + (place + i) % half, me).start()
+            return carry
+
+        def beside(i, carry):
+            copy1(r, side * half + (place + 1 + i) % half, me).start()
+            return carry
+
+        lax.fori_loop(0, half, across, 0)
+        lax.fori_loop(0, half - 1, beside, 0)
+        recv1[r * n + me] = send1[r * half + place]
+    for get in gets[1:]:
         get.wait()
 
     def one_pair(q):
@@ -265,46 +257,70 @@
         return jnp.concatenate([re, im], axis=1)
 
     step = 16 // ch
-    size = pairs_out * ch
-
-    def chunk(k, carry):
-        c = quarter(k)
-        for j in range(group * pairs_out // step):
-            q = c * (group * pairs_out) + j * step
-            cross[j * 16 : (j + 1) * 16, :] = jnp.concatenate(
-                [one_pair(q + i) for i in range(step)], axis=0
-            ).astype(jnp.bfloat16)
-        lags = jnp.dot(cross[...], wv[...], preferred_element_type=jnp.float32)
-        for g in range(group):
-            d = c * group + g
-            mine = lags[g * size : (g + 1) * size]
-            for m in range(BULK // LANES):
-                send2[d, m * size : (m + 1) * size, :] = mine[
-                    :, m * LANES : (m + 1) * LANES
-                ].astype(jnp.bfloat16)
-            rest = mine[:, BULK:]
+
+    for r in range(2):
+        for k in (3, 2, 1, 0):
+            c = quarter(k)
+            for g in range(group):
+                src = c * group + g
+
+                @pl.when(src != me)
+                def _():
+                    copy1(r, src, src).wait_recv()
+
+            got = recv1[pl.ds(r * n + c * group, group)].reshape(group * rows, WIN)
+            full = jnp.dot(got, fv[...], preferred_element_type=jnp.float32)
+            for g in range(group):
+                p = c * (group // seg_count) + g // seg_count
+                for b in range(blk_dev):
+                    at = g * rows + b * ch
+                    spec[p * blk_dev + b, g % seg_count] = full[at : at + ch]
+
+        def chunk(k, carry):
+            c = quarter(k)
+            for j in range(group * pairs_out // step):
+                q = c * (group * pairs_out) + j * step
+                cross[j * 16 : (j + 1) * 16, :] = jnp.concatenate(
+                    [one_pair(q + i) for i in range(step)], axis=0
+                ).astype(jnp.bfloat16)
+            lags = jnp.dot(cross[...], wv[...], preferred_element_type=jnp.float32)
             lane = lax.broadcasted_iota(jnp.int32, (size // 2, LANES), 1)
-            send2[d, BULK // LANES * size :, :] = jnp.where(
-                lane < TAIL, rest[: size // 2], rest[size // 2 :]
-            ).astype(jnp.bfloat16)
-
-            @pl.when(d != me)
-            def _():
-                copy2(d, me).start()
-
-        return carry
-
-    lax.fori_loop(0, 4, chunk, 0)
-    recv2[me] = send2[me]
-
-    def arrive2(i, carry):
-        src = (me + 1 + i) % n
-        copy2(src, src).wait_recv()
-        copy1(src, src).wait_send()
-        copy2(src, src).wait_send()
-        return carry
-
-    lax.fori_loop(0, n - 1, arrive2, 0)
+            for g in range(group):
+                d = c * group + g
+                to = r * half + d % half
+                mine = lags[g * size : (g + 1) * size]
+                for m in range(BULK // LANES):
+                    send2[to, m * size : (m + 1) * size, :] = mine[
+                        :, m * LANES : (m + 1) * LANES
+                    ].astype(jnp.bfloat16)
+                rest = mine[:, BULK:]
+                send2[to, BULK // LANES * size :, :] = jnp.where(
+                    lane < TAIL, rest[: size // 2], rest[size // 2 :]
+                ).astype(jnp.bfloat16)
+
+                @pl.when(d != me)
+                def _():
+                    copy2(r, d, me).start()
+
+            return carry
+
+        lax.fori_loop(2, 4, chunk, 0)
+        recv2[place * 2 + r] = send2[r * half + place]
+
+    for r in range(2):
+
+        def arrive2(i, carry):
+            src = side * half + (place + 1 + i) % half
+            copy2(r, src, src).wait_recv()
+            copy2(r, src, src).wait_send()
+            return carry
+
+        def sent1(i, carry):
+            copy1(r, (me + 1 + i) % n, me).wait_send()
+            return carry
+
+        lax.fori_loop(0, half - 1, arrive2, 0)
+        lax.fori_loop(0, n - 1, sent1, 0)
 
 
 def layout_kernel(n, ch, r_ref, o_hbm, ov, sems):
@@ -342,7 +358,7 @@
     any_spec = pl.BlockSpec(memory_space=pl.ANY)
     parts = pl.pallas_call(
         functools.partial(exchange_kernel, pair_count, seg_count, blk_dev, pairs_out, ch),
-        out_shape=jax.ShapeDtypeStruct((n, message, LANES), jnp.bfloat16),
+        out_shape=pltpu.VMEM((n, message, LANES), jnp.bfloat16),
         in_specs=[any_spec] * 5,
         out_specs=pl.BlockSpec(memory_space=pltpu.VMEM),
         scratch_shapes=[
@@ -353,13 +369,13 @@
             pltpu.VMEM(inverse.shape, jnp.bfloat16),
             pltpu.VMEM((WIN, WIN), jnp.bfloat16),
             pltpu.VMEM((n, rows, WIN), jnp.bfloat16),
-            pltpu.VMEM((n, rows, WIN), jnp.bfloat16),
+            pltpu.VMEM((2 * n, rows, WIN), jnp.bfloat16),
             pltpu.VMEM((nblk, seg_count, ch, N), jnp.float32),
             pltpu.VMEM((group * pairs_out * ch, N), jnp.bfloat16),
             pltpu.VMEM((n, message, LANES), jnp.bfloat16),
             pltpu.SemaphoreType.DMA((5,)),
-            pltpu.SemaphoreType.DMA((n,)),
-            pltpu.SemaphoreType.DMA((n,)),
+            pltpu.SemaphoreType.DMA((2 * n,)),
+            pltpu.SemaphoreType.DMA((2 * n,)),
             pltpu.SemaphoreType.DMA((n,)),
             pltpu.SemaphoreType.DMA((n,)),
         ],

time: 27.4 us -> 25.6 us (0.934)
  the two profiles are of different devices: /device:TPU:9 before, /device:TPU:1 now
where the time goes in v3:
time: 25.6 us; the launch traced here: 25.4 us
  Pallas kernels  25.4 us (99%)
    pallas_call x1, Pallas kernels, channel_shards(): pl.pallas_call(functools.partial(exchange_kernel, pair_count, seg_count,...  24.3 us
    pallas_call x1, Pallas kernels, channel_shards(): pl.pallas_call(functools.partial(layout_kernel, n, ch), out_shape=jax.Sha...  1.06 us

profile of v3, /device:TPU:1, one launch (start us, length us, event | category | flops | bytes accessed | tf_op | source)
XLA Modules:
  0.0 25.4 jit_solution(12744305451642257708)
XLA Ops:
  0.0 24.3 %exchange.1.r_ref = bf16[16,112,128]{2,1,0:T(8,128)(2,1)S(1)} custom-call(f32[256,512]{1,0:T(8,128)} %x_hbm.1, s32[16]{0:T(128)} %slot_hbm.1, s32[2,64]{1,0:T(2,128)} %bitcast.1, bf16[512,768]{1,0:T(8,128)(2,1)} %constant.4.clone.f_hbm, bf16[768,512]{1,0:T(8,128)(2,1)} %constant.5.clone.w_hbm), custom_call_target="tpu_custom_call" | custom-call | tf_op jit(solution)/shard_map/exchange/pallas_call | solution.py:359
  24.4 1.1 %layout.1 = f32[4,400,128]{2,1,0:T(8,128)} custom-call(bf16[16,112,128]{2,1,0:T(8,128)(2,1)S(1)} %exchange.1.r_ref), custom_call_target="tpu_custom_call" | custom-call | tf_op jit(solution)/shard_map/layout/pallas_call | solution.py:387
